TPU v7x, 32 devices: a whole 2x2x4 slice. The times are simulated.
32 devices in a mesh: row: 8 (over y, x, core), col: 4 (over z).
Axes of the slice: x: 2, y: 2, z: 4, core: 2. Of those that a mesh axis runs over, the one named last changes fastest.
Arguments:
- trailing: float32 [16384, 16384], P('row', 'col'), may hold values from -12 to 12, as said below
- panel: float32 [16384, 256], P('row'), may hold values from -3 to 3, as said below
Outputs:
- updated: float32 [16384, 16384], P('row', 'col')
- band_block: float32 [256, 256], replicated
Inputs may be any that keep to these rules, and one draw needn't show every extreme that they name: trailing, read in global order, equals its transpose. Read in global order, the top 256 x 256 block of panel is 2 I plus entries of magnitude at most 6 / sqrt(16384), and the rows below have entries of magnitude at most 6 / sqrt(16384).
All inputs are finite; a program needn't handle non-finite values.
Results may differ from a plain program's by a relative error of at most 0.00011.
Values sent between devices are 32-bit elements; how exact they have to be, the bound alone decides.
A program may use at most 128 MiB of HBM per device.

v0:
```python
import jax
import jax.numpy as jnp
from jax import lax
from jax.sharding import PartitionSpec as P


def matmul(left, right):
    return jnp.dot(left, right, precision=lax.Precision.HIGHEST, preferred_element_type=jnp.float32)


def matmul_tn(left, right):
    return lax.dot_general(
        left,
        right,
        (((0,), (0,)), ((), ())),
        precision=lax.Precision.HIGHEST,
        preferred_element_type=jnp.float32,
    )


def matmul_nt(left, right):
    return lax.dot_general(
        left,
        right,
        (((1,), (1,)), ((), ())),
        precision=lax.Precision.HIGHEST,
        preferred_element_type=jnp.float32,
    )


def lu_unpivoted(matrix):
    order_size = matrix.shape[0]
    positions = jnp.arange(order_size)

    def eliminate(column, factors):
        below = positions > column
        column_values = lax.dynamic_slice_in_dim(factors, column, 1, 1)[:, 0]
        row_values = lax.dynamic_slice_in_dim(factors, column, 1, 0)[0]
        pivot_value = lax.dynamic_slice_in_dim(column_values, column, 1, 0)[0]
        multipliers = jnp.where(below, column_values / pivot_value, 0.0)
        pivot_row = jnp.where(below, row_values, 0.0)
        factors = factors - multipliers[:, None] * pivot_row[None, :]
        stored = jnp.where(below, multipliers, column_values)[:, None]
        return lax.dynamic_update_slice_in_dim(factors, stored, column, 1)

    factors = lax.fori_loop(0, order_size, eliminate, matrix)
    unit_lower = jnp.tril(factors, -1) + jnp.eye(order_size, dtype=matrix.dtype)
    return (unit_lower, jnp.triu(factors))


def cholesky_columns(matrix):
    order_size = matrix.shape[0]
    positions = jnp.arange(order_size)

    def factor_step(column, carry):
        remaining, factor = carry
        column_values = lax.dynamic_slice_in_dim(remaining, column, 1, 1)[:, 0]
        pivot_root = jnp.sqrt(lax.dynamic_slice_in_dim(column_values, column, 1, 0)[0])
        factor_col = jnp.where(positions >= column, column_values / pivot_root, 0.0)
        remaining = remaining - factor_col[:, None] * factor_col[None, :]
        factor = lax.dynamic_update_slice_in_dim(factor, factor_col[:, None], column, 1)
        return (remaining, factor)

    start = (matrix, jnp.zeros_like(matrix))
    return lax.fori_loop(0, order_size, factor_step, start)[1]


def inverse_lower(lower):
    order_size = lower.shape[0]
    identity = jnp.eye(order_size, dtype=jnp.float32)
    diagonal = jnp.diagonal(lower)
    nilpotent = jnp.tril(lower, -1) / diagonal[None, :]
    power = -nilpotent
    result = identity + power
    steps = max(order_size - 1, 1).bit_length() - 1
    for level in range(steps):
        power = matmul(power, power)
        result = matmul(result, identity + power)
    return result / diagonal[:, None]


def mirror(row_piece, col_count, col_index, band_size):
    group_ratio = lax.axis_size("row") // col_count
    blocks = row_piece.shape[0] // band_size
    gathered = lax.all_gather(row_piece, "row", axis=0, tiled=True)
    gathered = gathered.reshape(group_ratio, col_count, blocks, band_size, band_size)
    pieces = lax.dynamic_index_in_dim(gathered, col_index, 1, keepdims=False)
    return pieces.transpose(1, 0, 2, 3).reshape(group_ratio * row_piece.shape[0], band_size)


def shards(trailing, panel):
    col_count = lax.axis_size("col")
    row_index = lax.axis_index("row")
    col_index = lax.axis_index("col")
    band_size = panel.shape[1]
    identity = jnp.eye(band_size, dtype=jnp.float32)
    first_owner = (row_index == 0).astype(jnp.float32)
    gram_part = matmul_tn(panel, panel)
    top_part = panel[:band_size] * first_owner
    gram_total, top_rows = lax.psum((gram_part, top_part), "row")
    lower_chol = cholesky_columns(gram_total)
    chol_inverse = inverse_lower(lower_chol)
    ortho_rows = matmul_nt(panel, chol_inverse)
    ortho_top = matmul_nt(top_rows, chol_inverse)
    unit_lower, upper_tri = lu_unpivoted(identity + ortho_top)
    upper_inverse = inverse_lower(upper_tri.T).T
    unit_inverse = inverse_lower(unit_lower)
    shifted = ortho_rows.at[:band_size].add(identity * first_owner)
    reflectors = matmul(shifted, upper_inverse)
    tri_factor = matmul_nt(upper_tri, unit_inverse)
    refl_cols = mirror(reflectors, col_count, col_index, band_size)
    product_rows = lax.psum(matmul(trailing, refl_cols), "col")
    inner_gram = lax.psum(matmul_tn(reflectors, product_rows), "row")
    middle = matmul(matmul(tri_factor.T, inner_gram), tri_factor)
    update_rows = matmul(product_rows, tri_factor) - 0.5 * matmul(reflectors, middle)
    product_cols = lax.psum(matmul_tn(trailing, reflectors), "row")
    update_cols = matmul(product_cols, tri_factor) - 0.5 * matmul(refl_cols, middle)
    updated = trailing - matmul_nt(reflectors, update_cols) - matmul_nt(update_rows, refl_cols)
    return (updated, -lower_chol.T)


def solution(mesh):
    return jax.shard_map(
        shards,
        mesh=mesh,
        in_specs=(P("row", "col"), P("row", None)),
        out_specs=(P("row", "col"), P()),
        check_vma=False,
    )
```

profile of v0, /device:TPU:0, one launch (start us, length us, event | category | flops | bytes accessed | tf_op | source)
XLA Modules:
  0.0 1332.7 jit_solution(17506444548522829434)
XLA Ops:
  7.2 6.4 fusion.31
  13.6 1.7 slice_multiply_fusion
  15.7 57.2 %all-reduce.10.cloned.1.call-done = (f32[256,256]{1,0:T(8,128)}, f32[256,256]{1,0:T(8,128)}) async-done(((f32[256,256]{1,0:T(8,128)}, f32[256,256]{1,0:T(8,128)}), (f32[256,256]{1,0:T(8,128)}, f32[256,256]{1,0:T(8,128)})) %all-reduce.10.cloned.1.call-update) | async-done | bytes 524304 | tf_op jit(solution)/shard_map/psum | solution.py:100
  72.8 1.1 copy.22
  73.9 387.9 %while.39 = (s32[]{:T(128)}, f32[256,256]{0,1:T(8,128)S(1)}, f32[256,256]{0,1:T(8,128)S(1)}) while((s32[]{:T(128)}, f32[256,256]{0,1:T(8,128)S(1)}, f32[256,256]{0,1:T(8,128)S(1)}) %tuple.105), condition=%wide.region_2.3_spmd.clone.clone, body=%wide.region_1.0_spmd.clone.sunk.clone | while | flops 132355 | bytes 534125 | solution.py:65
  462.0 2.4 gather_fusion
  470.6 409.5 %while.40 = (s32[]{:T(128)}, f32[256,256]{0,1:T(8,128)S(1)}) while((s32[]{:T(128)}, f32[256,256]{0,1:T(8,128)S(1)}) %tuple.108), condition=%wide.region_5.6_spmd.clone.clone, body=%wide.region_4.5_spmd.clone.sunk.clone | while | flops 132355 | bytes 1058653 | solution.py:46
  472.8 0.7 reshape_select_fusion.13
  474.4 0.7 reshape_select_fusion.13
  477.6 0.7 reshape_select_fusion.13
  479.2 0.7 reshape_select_fusion.13
  482.4 0.7 reshape_select_fusion.13
  484.0 0.7 reshape_select_fusion.13
  485.6 0.7 reshape_select_fusion.13
  487.2 0.7 reshape_select_fusion.13
  488.8 0.7 reshape_select_fusion.13
  490.4 0.7 reshape_select_fusion.13
  492.0 0.7 reshape_select_fusion.13
  493.6 0.7 reshape_select_fusion.13
  495.2 0.7 reshape_select_fusion.13
  496.8 0.7 reshape_select_fusion.13
  498.4 0.7 reshape_select_fusion.13
  500.0 0.7 reshape_select_fusion.13
  503.2 0.7 reshape_select_fusion.13
  504.8 0.7 reshape_select_fusion.13
  508.0 0.7 reshape_select_fusion.13
  509.6 0.7 reshape_select_fusion.13
  512.8 0.7 reshape_select_fusion.13
  514.4 0.7 reshape_select_fusion.13
  516.0 0.7 reshape_select_fusion.13
  517.6 0.7 reshape_select_fusion.13
  519.2 0.7 reshape_select_fusion.13
  520.8 0.7 reshape_select_fusion.13
  522.4 0.7 reshape_select_fusion.13
  524.0 0.7 reshape_select_fusion.13
  525.6 0.7 reshape_select_fusion.13
  527.2 0.7 reshape_select_fusion.13
  528.8 0.7 reshape_select_fusion.13
  530.4 0.7 reshape_select_fusion.13
  533.6 0.7 reshape_select_fusion.13
  535.2 0.7 reshape_select_fusion.13
  538.4 0.7 reshape_select_fusion.13
  880.1 2.6 gather_fusion.1
  884.3 2.0 fusion.37
  889.8 1.1 fusion.17
  891.3 1.3 convolution_divide_fusion.1
  892.6 4.9 fusion.43
  897.9 2.3 gather_fusion.2
  902.8 84.1 %all-gather.2.cloned.1.call-done = f32[16384,256]{1,0:T(8,128)} async-done(((f32[2048,256]{1,0:T(8,128)}), f32[16384,256]{1,0:T(8,128)}) %all-gather.2.cloned.1.call-update) | async-done | bytes 16777232 | tf_op jit(solution)/shard_map/all_gather | solution.py:85
  986.9 2.6 constant_dynamic-slice_fusion.1
  990.0 1.9 copy-done.1
  991.9 67.3 %convolution_bitcast_fusion.1 = f32[2048,256]{0,1:T(8,128)} fusion(f32[4096,256]{1,0:T(8,128)S(1)} %bitcast.133, f32[2048,4096]{1,0:T(8,128)} %param.8), kind=kOutput, calls=%fused_computation.22 | convolution fusion | flops 25769803776 | bytes 39845888 | tf_op jit(solution)/shard_map/dot_general | solution.py:8
  1059.4 1.1 fusion.20
  1061.0 34.3 %convolution_bitcast_fusion = f32[4096,256]{0,1:T(8,128)} fusion(f32[2048,256]{1,0:T(8,128)S(1)} %copy-done, f32[2048,4096]{1,0:T(8,128)} %param.8), kind=kOutput, calls=%fused_computation.19 | convolution fusion | flops 25769803776 | bytes 39845888 | tf_op jit(solution)/shard_map/dot_general | solution.py:12
  1095.3 50.7 %all-reduce.6.cloned.1.call-done = f32[2048,256]{0,1:T(8,128)} async-done(((f32[2048,256]{0,1:T(8,128)}), f32[2048,256]{0,1:T(8,128)}) %all-reduce.6.cloned.1.call-update) | async-done | bytes 2097168 | tf_op jit(solution)/shard_map/psum | solution.py:112
  1146.0 5.9 fusion.50
  1151.9 0.7 negate_bitcast_fusion
  1155.9 5.0 fusion.54
  1160.9 74.2 %all-reduce.8.cloned.1.call-done = (f32[4096,256]{0,1:T(8,128)}, f32[256,256]{1,0:T(8,128)}) async-done(((f32[4096,256]{0,1:T(8,128)}, f32[256,256]{1,0:T(8,128)}), (f32[4096,256]{0,1:T(8,128)}, f32[256,256]{1,0:T(8,128)})) %all-reduce.8.cloned.1.call-update) | async-done | bytes 4456464 | tf_op jit(solution)/shard_map/psum | solution.py:116
  1235.2 8.8 fusion.49
  1245.0 3.2 fusion.5
  1248.2 3.4 fusion.4
  1251.6 31.2 %fusion.53 = f32[2048,4096]{1,0:T(8,128)} fusion(f32[2048,256]{1,0:T(8,128)S(1)} %copy-done, f32[4096,256]{1,0:T(8,128)S(1)} %fusion.4), kind=kOutput, calls=%fused_computation.112 | convolution fusion | flops 25769803776 | bytes 39845888 | tf_op jit(solution)/shard_map/dot_general | solution.py:22
  1282.8 43.1 %subtract_subtract_fusion = f32[2048,4096]{1,0:T(8,128)} fusion(f32[2048,4096]{1,0:T(8,128)} %param.8, f32[2048,4096]{1,0:T(8,128)} %fusion.53, f32[2048,256]{1,0:T(8,128)} %fusion.5, f32[4096,256]{1,0:T(8,128)} %bitcast.134), kind=kOutput, calls=%fused_computation.16 | convolution fusion | flops 25786580992 | bytes 106954752 | tf_op jit(solution)/shard_map/dot_general | solution.py:22
  (3377 shorter events, 589.5 us)
Async XLA Ops:
  7.2 65.7 %all-reduce.10.cloned.1.call-start = ((), (), s32[]{:S(2)}) async-start(), calls=%async_computation.3 | async-start | bytes 1048576 | tf_op jit(solution)/shard_map/psum | solution.py:100
  15.3 971.6 %all-gather.2.cloned.1.call-start = ((), (), s32[]{:S(2)}) async-start(), calls=%async_computation | async-start | bytes 18874368 | tf_op jit(solution)/shard_map/all_gather | solution.py:85
  468.1 2.0 copy-start.7
  882.7 1.6 copy-start.3
  897.6 248.4 %all-reduce.6.cloned.1.call-start = ((), (), s32[]{:S(2)}) async-start(), calls=%async_computation.1 | async-start | bytes 4194304 | tf_op jit(solution)/shard_map/psum | solution.py:112
  990.0 2.0 copy-start.1
  1059.3 1.7 copy-start
  1059.3 175.8 %all-reduce.8.cloned.1.call-start = ((), (), s32[]{:S(2)}) async-start(), calls=%async_computation.2 | async-start | bytes 8912896 | tf_op jit(solution)/shard_map/psum | solution.py:116
  1151.9 1.0 copy-start.6
  1153.7 2.2 copy-start.5
  1235.2 8.8 copy-start.8
  1235.2 9.8 copy-start.4
  1245.0 3.2 copy-start.2
Sparse Core Ops, SparseCore 0:
  15.4 57.3 all-reduce.9
  897.7 89.1 all-gather.1
  1059.4 86.5 all-reduce.5
  1152.0 83.0 all-reduce.7
where the time goes:
time: 1350 us; the launch traced here: 1330 us
  local copies, waits for them, and re-layouts  372 us (28%)
  waiting for transfers between devices  266 us (20%)
  other arithmetic  238 us (18%)
  matrix products  237 us (18%)
  loops' own time  205 us (15%)
  between operations  14.7 us (1%)
    another operation x1, loops' own time, cholesky_columns(): return lax.fori_loop(0, order_size, factor_step, start)[1]  191 us
    select_n x256, other arithmetic, eliminate(): stored = jnp.where(below, multipliers, column_values)[:, None]  168 us
    dynamic_slice x256, local copies, waits for them, and re-layouts, factor_step(): lax.dynamic_slice_in_dim(column_values, column, 1, 0)[0]  151 us
    dynamic_slice x256, local copies, waits for them, and re-layouts, eliminate(): pivot_value = lax.dynamic_slice_in_dim(column_values, column, 1, 0)[0]  151 us
    dot_general x50, matrix products, matmul(): jnp.dot(left, right, precision=lax.Precision.HIGHEST, preferred_element_t...  113 us
    all_gather x1, waiting for transfers between devices, mirror(): gathered = lax.all_gather(row_piece, 'row', axis=0, tiled=True)  84.1 us
    dot_general x5, matrix products, matmul_nt(): lax.dot_general(left, right, (((1,), (1,)), ((), ())), precision=lax.Prec...  77.2 us
    psum x1, waiting for transfers between devices, shards(): product_cols = lax.psum(matmul_tn(trailing, reflectors), 'row')  74.2 us
  transfers between devices with their start and end apart: 4, of which 4 were waited for; matrix products, arithmetic and copies ran while one was open for 4% of the time, Pallas kernels for 0%

commit v1 on v0

v1 whole, which is shorter than its diff:
```python
import jax
import jax.numpy as jnp
from jax import lax
from jax.experimental import pallas as pl
from jax.experimental.pallas import tpu as pltpu
from jax.sharding import PartitionSpec as P

FULL = lax.Precision.HIGHEST
THREE = lax.Precision.HIGH
STEP = 64


def contract(left, right, dims, precision):
    return lax.dot_general(left, right, ((dims[:1], dims[1:]), ((), ())), precision=precision, preferred_element_type=jnp.float32)


def matmul(left, right, precision=FULL):
    return contract(left, right, (1, 0), precision)


def matmul_tn(left, right, precision=FULL):
    return contract(left, right, (0, 0), precision)


def matmul_nt(left, right, precision=FULL):
    return contract(left, right, (1, 1), precision)


def chol_kernel(gram_ref, upper_ref, work):
    size = gram_ref.shape[0]
    work[...] = gram_ref[...]
    sub = lax.broadcasted_iota(jnp.int32, (STEP, 2 * STEP), 0)
    lane = lax.broadcasted_iota(jnp.int32, (STEP, 2 * STEP), 1)
    eye = (lax.broadcasted_iota(jnp.int32, (STEP, STEP), 0) == lax.broadcasted_iota(jnp.int32, (STEP, STEP), 1)).astype(jnp.float32)
    row_pos = lax.broadcasted_iota(jnp.int32, (STEP, size), 0)
    col_pos = lax.broadcasted_iota(jnp.int32, (STEP, size), 1)
    for base in range(0, size, STEP):
        rows = work[base:base + STEP, :]
        pair = jnp.concatenate([rows[:, base:base + STEP], eye], axis=1)
        for j in range(STEP):
            col = jnp.broadcast_to(pair[:, j:j + 1], (STEP, 2 * STEP))
            pivot = col[j:j + 1, :]
            scale = lax.rsqrt(pivot)
            scale = scale * (1.5 - 0.5 * pivot * scale * scale)
            row = pair[j:j + 1, :] * scale
            reduced = pair - (col * scale) * row
            pair = jnp.where(sub > j, reduced, jnp.where(sub == j, row, pair))
        solved = matmul(pair[:, STEP:], rows)
        solved = jnp.where(col_pos >= row_pos + base, solved, 0.0)
        upper_ref[base:base + STEP, :] = solved
        if base + STEP < size:
            work[...] = work[...] - matmul_tn(solved, solved)


def inverse_kernel(matrix_ref, out_ref):
    size = matrix_ref.shape[0]
    out_ref[...] = matrix_ref[...]
    sub = lax.broadcasted_iota(jnp.int32, (STEP, STEP), 0)
    lane = lax.broadcasted_iota(jnp.int32, (STEP, STEP), 1)
    for base in range(0, size, STEP):
        rows = out_ref[base:base + STEP, :]
        block = rows[:, base:base + STEP]
        for j in range(STEP):
            col = jnp.broadcast_to(block[:, j:j + 1], (STEP, STEP))
            inv = 1.0 / col[j:j + 1, :]
            row = jnp.where(lane[:1] == j, inv, block[j:j + 1, :] * inv)
            rest = jnp.where(lane == j, 0.0, block) - col * row
            block = jnp.where(sub == j, row, rest)
        cols = out_ref[:, base:base + STEP]
        solved = matmul(block, rows)
        lanes = lax.broadcasted_iota(jnp.int32, (STEP, size), 1)
        inside = (lanes >= base) & (lanes < base + STEP)
        pieces = [jnp.zeros((STEP, STEP), jnp.float32)] * (size // STEP)
        pieces[base // STEP] = block
        solved = jnp.where(inside, jnp.concatenate(pieces, axis=1), solved)
        lanes = lax.broadcasted_iota(jnp.int32, (size, size), 1)
        kept = jnp.where((lanes >= base) & (lanes < base + STEP), 0.0, out_ref[...])
        out_ref[...] = kept - matmul(cols, solved)
        out_ref[base:base + STEP, :] = solved


def small_call(kernel, matrix, scratch, name):
    size = matrix.shape[0]
    return pl.pallas_call(
        kernel,
        out_shape=jax.ShapeDtypeStruct((size, size), jnp.float32),
        in_specs=[pl.BlockSpec(memory_space=pltpu.VMEM)],
        out_specs=pl.BlockSpec(memory_space=pltpu.VMEM),
        scratch_shapes=scratch,
        compiler_params=pltpu.CompilerParams(vmem_limit_bytes=16 * 1024 * 1024),
        cost_estimate=pl.CostEstimate(flops=40_000_000_000, bytes_accessed=8 * size * size, transcendentals=0),
        name=name,
    )(matrix)


def cholesky_upper(matrix):
    return small_call(chol_kernel, matrix, [pltpu.VMEM(matrix.shape, jnp.float32)], "cholesky_upper")


def inverse(matrix):
    return small_call(inverse_kernel, matrix, [], "block_inverse")


def mirror(row_piece, col_count, col_index, band_size):
    group_ratio = lax.axis_size("row") // col_count
    blocks = row_piece.shape[0] // band_size
    gathered = lax.all_gather(row_piece, "row", axis=0, tiled=True)
    gathered = gathered.reshape(group_ratio, col_count, blocks, band_size, band_size)
    pieces = lax.dynamic_index_in_dim(gathered, col_index, 1, keepdims=False)
    return pieces.transpose(1, 0, 2, 3).reshape(group_ratio * row_piece.shape[0], band_size)


def shards(trailing, panel):
    col_count = lax.axis_size("col")
    row_index = lax.axis_index("row")
    col_index = lax.axis_index("col")
    band_size = panel.shape[1]
    row_first = (row_index == 0).astype(jnp.float32)
    col_first = (col_index == 0).astype(jnp.float32)
    first = jnp.concatenate([matmul_tn(panel, panel), panel[:band_size] * row_first], axis=0)
    first = lax.psum(first, "row")
    gram_total, top_rows = first[:band_size], first[band_size:]
    panel_cols = mirror(panel, col_count, col_index, band_size)
    upper = cholesky_upper(gram_total)
    v_rows = panel.at[:band_size].add(upper * row_first)
    v_cols = panel_cols.at[:band_size].add(upper * col_first)
    part_cols = matmul_tn(trailing, v_rows, THREE)
    x_cols = lax.psum(part_cols, "row")
    part_rows = matmul(trailing, v_cols, THREE)
    x_rows = lax.psum(part_rows, "col")
    inner = lax.psum(matmul_tn(v_rows, part_rows), ("row", "col"))
    core = inverse(gram_total + matmul_tn(upper, top_rows))
    half = 0.5 * matmul_nt(matmul(core, inner), core)
    w_rows = matmul_nt(x_rows, core, THREE) - matmul(v_rows, half, THREE)
    w_cols = matmul_nt(x_cols, core, THREE) - matmul(v_cols, half, THREE)
    left = jnp.concatenate([v_rows, w_rows], axis=1)
    right = jnp.concatenate([w_cols, v_cols], axis=1)
    return (trailing - matmul_nt(left, right, THREE), -upper)


def solution(mesh):
    return jax.shard_map(
        shards,
        mesh=mesh,
        in_specs=(P("row", "col"), P("row", None)),
        out_specs=(P("row", "col"), P()),
        check_vma=False,
    )
```

time: 1350 us -> 570 us (0.42); the launches traced: 1330 us -> 567 us
  local copies, waits for them, and re-layouts: 372 us -> 8.73 us
  other arithmetic: 238 us -> 1.69 us
  loops' own time: 205 us -> 0 us
  matrix products: 237 us -> 127 us
  waiting for transfers between devices: 266 us -> 364 us
  Pallas kernels: 0 us -> 50.7 us
    dynamic_slice x512 -> x0, local copies, waits for them, and re-layouts: 302 us -> none  [the longest x256 151 us: factor_step(): lax.dynamic_slice_in_dim(column_values, column, 1, 0)[0]]
    another operation x2 -> x0, loops' own time: 205 us -> none  [the longest x1 191 us: cholesky_columns(): return lax.fori_loop(0, order_size, factor_step, start)[1]]
    select_n x1024 -> x0, other arithmetic: 176 us -> none  [the longest x256 168 us: eliminate(): stored = jnp.where(below, multipliers, column_values)[:, None]]
    psum x3 -> x4, waiting for transfers between devices: 182 us -> 298 us  [the longest x1 86.2 us: shards(): x_rows = lax.psum(part_rows, 'col')]
    dot_general x58 -> x12, matrix products: 237 us -> 127 us  [contract(): lax.dot_general(left, right, ((dims[:1], dims[1:]), ((), ())), precision=...]
    sub x512 -> x0, other arithmetic: 57.3 us -> none  [the longest x256 28.7 us: factor_step(): remaining = remaining - factor_col[:, None] * factor_col[None, :]]
    pallas_call x0 -> x2, Pallas kernels: none -> 50.7 us  [small_call(): pl.pallas_call(kernel, out_shape=jax.ShapeDtypeStruct((size, size), jnp.f...]
    while x258 -> x0, local copies, waits for them, and re-layouts: 33.1 us -> none
  transfers between devices with their start and end apart: 4 -> 5, of which waited for: 4 -> 5; matrix products, arithmetic and copies ran while one was open for 4% -> 5% of each run, Pallas kernels for 0% -> 9%
where the time goes in v1:
time: 570 us; the launch traced here: 567 us
  waiting for transfers between devices  364 us (64%)
  matrix products  127 us (22%)
  Pallas kernels  50.7 us (9%)
  between operations  14.1 us (2%)
  local copies, waits for them, and re-layouts  8.73 us (2%)
    dot_general x12, matrix products, contract(): lax.dot_general(left, right, ((dims[:1], dims[1:]), ((), ())), precision=...  127 us
    psum x1, waiting for transfers between devices, shards(): x_rows = lax.psum(part_rows, 'col')  86.2 us
    psum x1, waiting for transfers between devices, shards(): x_cols = lax.psum(part_cols, 'row')  77.8 us
    psum x1, waiting for transfers between devices, shards(): inner = lax.psum(matmul_tn(v_rows, part_rows), ('row', 'col'))  77.2 us
    all_gather x1, waiting for transfers between devices, mirror(): gathered = lax.all_gather(row_piece, 'row', axis=0, tiled=True)  65 us
    psum x1, waiting for transfers between devices, shards(): first = lax.psum(first, 'row')  56.6 us
    pallas_call x2, Pallas kernels, small_call(): pl.pallas_call(kernel, out_shape=jax.ShapeDtypeStruct((size, size), jnp.f...  50.7 us
  transfers between devices with their start and end apart: 5, of which 5 were waited for; matrix products, arithmetic and copies ran while one was open for 5% of the time, Pallas kernels for 9%

profile of v1, /device:TPU:0, one launch (start us, length us, event | category | flops | bytes accessed | tf_op | source)
XLA Modules:
  0.0 566.8 jit_solution(7214939419763495206)
XLA Ops:
  7.2 0.0 all-reduce.5.cloned.1.call-start
  7.2 1.6 copy.12
  8.8 0.0 copy-start
  8.8 3.5 fusion.10
  12.3 0.8 pad_maximum_fusion
  13.1 0.0 all-reduce.5.cloned.1.call-update
  13.2 0.0 all-gather.2.cloned.1.call-start
  13.2 0.0 copy-done
  13.2 0.7 all-gather.2.cloned.1.call-update
  13.9 0.0 all-reduce.9.cloned.1.call-start
  14.0 56.6 %all-reduce.5.cloned.1.call-done = f32[512,256]{1,0:T(8,128)} async-done(((f32[512,256]{1,0:T(8,128)}), f32[512,256]{1,0:T(8,128)}) %all-reduce.5.cloned.1.call-update) | async-done | bytes 524304 | tf_op jit(solution)/shard_map/psum | solution.py:121
  70.6 1.0 slice.49.gram_ref
  71.5 25.8 %cholesky_upper.1 = f32[256,256]{1,0:T(8,128)S(1)} custom-call(f32[256,256]{1,0:T(8,128)S(1)} %slice.49.gram_ref), custom_call_target="tpu_custom_call" | custom-call | flops 40000000000 | bytes 524288 | tf_op jit(solution)/shard_map/cholesky_upper/pallas_call | solution.py:84
  97.4 65.0 %all-gather.2.cloned.1.call-done = f32[16384,256]{1,0:T(8,128)} async-done(((f32[2048,256]{1,0:T(8,128)}), f32[16384,256]{1,0:T(8,128)}) %all-gather.2.cloned.1.call-update) | async-done | bytes 16777232 | tf_op jit(solution)/shard_map/all_gather | solution.py:107
  162.4 2.6 constant_dynamic-slice_fusion
  165.1 0.0 copy-start.1
  165.1 0.4 copy.4
  165.5 1.2 copy-done.1
  166.6 0.9 fusion.9
  167.5 0.0 copy-start.2
  167.5 1.9 copy-done.2
  169.4 42.7 %fusion.11 = f32[256,2048]{1,0:T(8,128)} fusion(f32[4096,256]{1,0:T(8,128)} %copy-done.2, f32[2048,4096]{1,0:T(8,128)} %param.6), kind=kOutput, calls=%fused_computation.22 | convolution fusion | flops 12884901888 | bytes 39845888 | tf_op jit(solution)/shard_map/dot_general | solution.py:14
  212.1 0.0 copy-start.4
  212.1 5.8 %fusion.13 = f32[256,256]{1,0:T(8,128)} fusion(f32[2048,256]{1,0:T(8,128)S(1)} %get-tuple-element.28, f32[256,2048]{1,0:T(8,128)} %fusion.11), kind=kOutput, calls=%fused_computation.24 | convolution fusion | flops 1610612736 | bytes 4456448 | tf_op jit(solution)/shard_map/dot_general | solution.py:14
  218.0 0.0 all-reduce.9.cloned.1.call-update
  218.0 0.0 all-reduce.7.cloned.1.call-start
  218.0 0.5 all-reduce.7.cloned.1.call-update
  218.6 0.0 all-reduce.11.cloned.1.call-start
  218.6 0.0 copy-done.4
  218.6 0.6 convolution_add_fusion.matrix_ref
  219.2 22.0 %convolution_bitcast_fusion = f32[4096,256]{0,1:T(8,128)} fusion(f32[2048,256]{1,0:T(8,128)S(1)} %get-tuple-element.28, f32[2048,4096]{1,0:T(8,128)} %param.6), kind=kOutput, calls=%fused_computation.5 | convolution fusion | flops 12884901888 | bytes 39845888 | tf_op jit(solution)/shard_map/dot_general | solution.py:14
  241.2 0.0 all-reduce.11.cloned.1.call-update
  241.2 24.8 %block_inverse.1 = f32[256,256]{1,0:T(8,128)S(1)} custom-call(f32[256,256]{1,0:T(8,128)S(1)} %convolution_add_fusion.matrix_ref), custom_call_target="tpu_custom_call" | custom-call | flops 40000000000 | bytes 524288 | tf_op jit(solution)/shard_map/block_inverse/pallas_call | solution.py:84
  266.1 77.2 %all-reduce.9.cloned.1.call-done = f32[256,256]{1,0:T(8,128)} async-done(((f32[256,256]{1,0:T(8,128)}), f32[256,256]{1,0:T(8,128)}) %all-reduce.9.cloned.1.call-update) | async-done | bytes 262160 | tf_op jit(solution)/shard_map/psum | solution.py:131
  343.3 1.3 fusion.14
  344.6 0.4 convolution_multiply_fusion
  345.0 86.2 %all-reduce.7.cloned.1.call-done = f32[2048,256]{0,1:T(8,128)} async-done(((f32[2048,256]{0,1:T(8,128)}), f32[2048,256]{0,1:T(8,128)}) %all-reduce.7.cloned.1.call-update) | async-done | bytes 2097168 | tf_op jit(solution)/shard_map/psum | solution.py:130
  431.2 3.4 fusion.12
  434.6 2.4 convolution_subtract_fusion.2
  437.0 77.8 %all-reduce.11.cloned.1.call-done = f32[4096,256]{0,1:T(8,128)} async-done(((f32[4096,256]{0,1:T(8,128)}), f32[4096,256]{0,1:T(8,128)}) %all-reduce.11.cloned.1.call-update) | async-done | bytes 4194320 | tf_op jit(solution)/shard_map/psum | solution.py:128
  514.9 0.0 copy-start.3
  514.9 5.9 %fusion.15 = f32[4096,256]{1,0:T(8,128)S(1)} fusion(f32[4096,256]{0,1:T(8,128)} %all-reduce.11.cloned.1.call-done, f32[256,256]{1,0:T(8,128)S(1)} %block_inverse.1), kind=kOutput, calls=%fused_computation.26 | convolution fusion | flops 1610612736 | bytes 8650752 | tf_op jit(solution)/shard_map/dot_general | solution.py:14
  520.8 0.0 copy-done.3
  520.8 3.8 convolution_subtract_fusion.1
  524.6 35.5 %convolution_subtract_fusion = f32[2048,4096]{1,0:T(8,128)} fusion(f32[2048,4096]{1,0:T(8,128)} %param.6, f32[4096,256]{1,0:T(8,128)} %copy-done.2, f32[4096,256]{1,0:T(8,128)} %convolution_subtract_fusion.1, f32[2048,256]{1,0:T(8,128)} %convolution_subtract_fusion.2, f32[2048,256]{1,0:T(8,128)S(1)} %get-tuple-element.28), kind=kOutput, calls=%fused_computation | convolution fusion | flops 25781338112 | bytes 79691776 | tf_op jit(solution)/shard_map/dot_general | solution.py:14
  (1 shorter events, 0.0 us)
Async XLA Ops:
  7.2 63.4 %all-reduce.5.cloned.1.call-start = ((), (), s32[]{:S(2)}) async-start(), calls=%async_computation | async-start | bytes 1048576 | tf_op jit(solution)/shard_map/psum | solution.py:121
  8.8 4.4 copy-start
  13.2 149.3 %all-gather.2.cloned.1.call-start = ((), (), s32[]{:S(2)}) async-start(), calls=%async_computation.1 | async-start | bytes 18874368 | tf_op jit(solution)/shard_map/all_gather | solution.py:107
  13.9 329.3 %all-reduce.9.cloned.1.call-start = ((), (), s32[]{:S(2)}) async-start(), calls=%async_computation.3 | async-start | bytes 524288 | tf_op jit(solution)/shard_map/psum | solution.py:131
  165.1 1.6 copy-start.1
  167.5 1.9 copy-start.2
  212.1 6.5 %copy-start.4 = (f32[512,256]{1,0:T(8,128)S(1)}, f32[512,256]{1,0:T(8,128)}, u32[]{:S(2)}) copy-start(f32[512,256]{1,0:T(8,128)} %all-reduce.5.cloned.1.call-done) | copy-start | bytes 1572868
  218.0 213.2 %all-reduce.7.cloned.1.call-start = ((), (), s32[]{:S(2)}) async-start(), calls=%async_computation.2 | async-start | bytes 4194304 | tf_op jit(solution)/shard_map/psum | solution.py:130
  218.6 296.3 %all-reduce.11.cloned.1.call-start = ((), (), s32[]{:S(2)}) async-start(), calls=%async_computation.4 | async-start | bytes 8388608 | tf_op jit(solution)/shard_map/psum | solution.py:128
  514.9 6.0 %copy-start.3 = (f32[4096,256]{1,0:T(8,128)S(1)}, f32[4096,256]{1,0:T(8,128)}, u32[]{:S(2)}) copy-start(f32[4096,256]{1,0:T(8,128)} %copy-done.2) | copy-start | bytes 12582916
Sparse Core Ops, SparseCore 0:
  13.3 57.2 all-reduce.4
  73.2 89.1 all-gather.1
  218.1 125.1 all-reduce.8
  345.6 85.5 all-reduce.6
  434.9 79.9 all-reduce.10
